TPU v7x, 128 devices: a whole 4x4x4 slice. The times are simulated.
128 devices in a mesh: blk: 8 (over z_lo, x), cd: 16 (over y, z_hi, core).
Axes of the slice: x: 4, y: 4, z: 4 (z_hi: 2, z_lo: 2; z = z_hi * 2 + z_lo), core: 2. Of those that a mesh axis runs over, the one named last changes fastest.
Arguments:
- integrals: float32 [256, 589824], P('blk', 'cd'), may hold values from -0.0078125 to 0.0078125
- tau: float32 [1024, 589824], P('blk', 'cd'), may hold values from -6 to 6
- singles: float32 [128, 768], replicated, may hold values from -0.5 to 0.5
- doubles: float32 [1024, 2, 768], P('blk', None, 'cd'), may hold values from -6 to 6
Outputs:
- updated: float32 [1024, 2, 768], P('blk', None, 'cd')
All inputs are finite; a program needn't handle non-finite values.
Results may differ from a plain program's by a relative error of at most 0.000088.
Values sent between devices are 32-bit elements; how exact they have to be, the bound alone decides.
A program may use at most 128 MiB of HBM per device.

v0:
```python
import math

import jax
import jax.numpy as jnp
from jax import lax
from jax.sharding import PartitionSpec as P


def on_device(integrals, tau, singles, doubles):
    pairs = tau.shape[0]
    ka_dev = integrals.shape[0]
    ka_all = ka_dev * lax.axis_size("blk")
    n_occ = singles.shape[0]
    a_win = ka_all // n_occ
    width = doubles.shape[2]
    part = lax.dot_general(
        tau,
        lax.all_gather(integrals, "blk", axis=0, tiled=True),
        (((1,), (1,)), ((), ())),
        precision=lax.Precision.HIGHEST,
        preferred_element_type=jnp.float32,
    )
    zeta_part = part.reshape(pairs, a_win, n_occ)
    zeta = lax.psum(zeta_part, "cd")
    columns = lax.dynamic_slice_in_dim(singles, lax.axis_index("cd") * width, width, 1)
    folded = jnp.einsum("pak,kb->pab", zeta, columns, precision=lax.Precision.HIGHEST)
    side = math.isqrt(pairs // 2)
    shaped = folded.reshape(2, side, side, a_win, width)
    swapped = jnp.transpose(shaped[::-1], (0, 2, 1, 3, 4)).reshape(pairs, a_win, width)
    return doubles - (folded + swapped)


def solution(mesh):
    placed = (P("blk", "cd"), P("blk", "cd"), P(), P("blk", None, "cd"))
    return jax.shard_map(
        on_device, mesh=mesh, in_specs=placed, out_specs=P("blk", None, "cd"), check_vma=False
    )
```

profile of v0, /device:TPU:1, one launch (start us, length us, event | category | flops | bytes accessed | tf_op | source)
XLA Modules:
  0.0 566.5 jit_solution(4173390900133024165)
XLA Ops:
  6.5 0.0 copy-start
  6.5 0.0 all-gather.2.cloned.1.call-start
  6.5 0.7 all-gather.2.cloned.1.call-update
  7.3 0.0 copy-start.1
  7.3 0.0 all-reduce.2.cloned.1.call-start
  7.3 372.1 %all-gather.2.cloned.1.call-done = f32[256,36864]{1,0:T(8,128)} async-done(((f32[32,36864]{1,0:T(8,128)}), f32[256,36864]{1,0:T(8,128)}) %all-gather.2.cloned.1.call-update) | async-done | bytes 37748752 | tf_op jit(solution)/shard_map/all_gather | solution.py:18
  379.4 42.1 %convolution_bitcast_fusion = f32[16,2,8,128]{3,2,1,0:T(8,128)S(1)} fusion(f32[128,36864]{1,0:T(8,128)} %param.5, f32[256,36864]{1,0:T(8,128)} %all-gather.2.cloned.1.call-done), kind=kOutput, calls=%fused_computation | convolution fusion | flops 14495514624 | bytes 56754176 | tf_op jit(solution)/shard_map/dot_general | solution.py:16
  421.6 0.7 copy.16
  422.2 0.0 all-reduce.2.cloned.1.call-update
  422.3 135.3 %all-reduce.2.cloned.1.call-done = f32[128,2,128]{2,0,1:T(8,128)} async-done(((f32[128,2,128]{2,0,1:T(8,128)}), f32[128,2,128]{2,0,1:T(8,128)}) %all-reduce.2.cloned.1.call-update) | async-done | bytes 131088 | tf_op jit(solution)/shard_map/psum | solution.py:24
  557.6 0.0 copy-done
  557.6 1.3 fusion
  558.8 0.1 copy.10
  559.0 0.1 copy.12
  559.1 0.0 copy-done.1
  559.1 0.6 add_subtract_fusion
  (2 shorter events, 0.0 us)
Async XLA Ops:
  6.5 551.0 %copy-start = (f32[128,768]{1,0:T(8,128)S(1)}, f32[128,768]{1,0:T(8,128)}, u32[]{:S(2)}) copy-start(f32[128,768]{1,0:T(8,128)} %param.6) | copy-start | bytes 1179652
  6.5 372.9 %all-gather.2.cloned.1.call-start = ((), (), s32[]{:S(2)}) async-start(), calls=%async_computation | async-start | bytes 42467328 | tf_op jit(solution)/shard_map/all_gather | solution.py:18
  7.3 551.8 %copy-start.1 = (f32[128,2,48]{0,2,1:T(8,128)S(1)}, f32[128,2,48]{0,2,1:T(8,128)}, u32[]{:S(2)}) copy-start(f32[128,2,48]{0,2,1:T(8,128)} %param.7) | copy-start | bytes 147460
  7.3 550.3 %all-reduce.2.cloned.1.call-start = ((), (), s32[]{:S(2)}) async-start(), calls=%async_computation.1 | async-start | bytes 262144 | tf_op jit(solution)/shard_map/psum | solution.py:24
Sparse Core Ops, SparseCore 0:
  9.0 370.3 all-gather.1
  422.4 135.1 all-reduce.1
where the time goes:
time: 567 us
  waiting for transfers between devices  508 us (90%)
  matrix products  43.4 us (8%)
  between operations  13.5 us (2%)
    all_gather x1, waiting for transfers between devices, on_device(): lax.all_gather(integrals, 'blk', axis=0, tiled=True)  372 us
    psum x1, waiting for transfers between devices, on_device(): zeta = lax.psum(zeta_part, 'cd')  135 us
    dot_general x1, matrix products, on_device(): lax.dot_general(tau, lax.all_gather(integrals, 'blk', axis=0, tiled=True)...  42.1 us
  transfers between devices with their start and end apart: 2, of which 2 were waited for; matrix products, arithmetic and copies ran while one was open for 0% of the time, Pallas kernels for 0%

commit v1 on v0

v1 whole, which is shorter than its diff:
```python
import jax
import jax.numpy as jnp
from jax import lax
from jax.experimental import pallas as pl
from jax.experimental.pallas import tpu as pltpu
from jax.sharding import PartitionSpec as P

MESH = pl.DeviceIdType.MESH
N_BLK, N_CD = 8, 16
ROWS, KA = 64, 32
JA, JB = 6, 3
OTHERS = ((1, 2), (0, 2), (0, 1))


def corner(b):
    x = b % 4
    return (((x + 1) // 2) % 2, x // 2, b // 4)


def block_of(v):
    return v[2] * 4 + v[1] * 2 + (v[0] + v[1]) % 2


def flipped(v, dims):
    return tuple((e + 1) % 2 if at in dims else e for at, e in enumerate(v))


def masked(v, d, m):
    return flipped(v, [o for bit, o in enumerate(OTHERS[d]) if (m >> bit) & 1])


def spot(v, d):
    return v[OTHERS[d][0]] + 2 * v[OTHERS[d][1]]


def tile_at(v, d, slot):
    new = list(v)
    new[OTHERS[d][0]] = slot % 2
    new[OTHERS[d][1]] = slot // 2
    return block_of(new)


def halves(x):
    high = x.astype(jnp.bfloat16)
    return high, (x - high.astype(jnp.float32)).astype(jnp.bfloat16)


def product(a, b, dims):
    a_high, a_low = halves(a)
    b_high, b_low = halves(b)

    def dot(l, r):
        return lax.dot_general(l, r, (dims, ((), ())), preferred_element_type=jnp.float32)

    return dot(a_high, b_high) + (dot(a_high, b_low) + dot(a_low, b_high))


def kernel(
    tau, integrals, singles, out,
    stage, sent, pairs, slabs, zeta, parts, summed, tiles, whole, columns, folded,
    stage_sem, own_sem, a_send, a_recv, b_send, b_recv, f_send, f_recv,
    s1, r1, s2, r2, s3, r3,
):
    b, c = lax.axis_index("blk"), lax.axis_index("cd")
    v = corner(b)
    depth = integrals.shape[1] // 12
    ka, kb = depth // JA, depth // JB
    width = singles.shape[1] // N_CD

    def base(d, m):
        return (d * 4 + spot(masked(v, d, m), d)) * depth

    def load(step, slot):
        j, d = step // 3, step % 3
        return [
            pltpu.make_async_copy(
                tau.at[:, pl.ds(pl.multiple_of(load_base(d, m) + j * ka, 128), ka)],
                stage.at[slot, m],
                stage_sem.at[slot, m],
            )
            for m in range(4)
        ]

    def load_base(d, m):
        if isinstance(d, int):
            return base(d, m)
        return jnp.where(d == 0, base(0, m), jnp.where(d == 1, base(1, m), base(2, m)))

    for copy in load(0, 0):
        copy.start()

    barrier = pltpu.get_barrier_semaphore()
    for o in range(1, N_BLK):
        pl.semaphore_signal(barrier, inc=1, device_id=((b + o) % N_BLK, c), device_id_type=MESH)
    for o in range(1, N_CD):
        pl.semaphore_signal(barrier, inc=1, device_id=(b, (c + o) % N_CD), device_id_type=MESH)
    pl.semaphore_wait(barrier, N_BLK + N_CD - 2)

    def b_copy(d, j, m):
        return pltpu.make_async_remote_copy(
            src_ref=integrals.at[:, pl.ds(pl.multiple_of(base(d, m) + j * kb, 128), kb)],
            dst_ref=slabs.at[d, j, b],
            send_sem=b_send.at[d, j, m],
            recv_sem=b_recv.at[d, j, m],
            device_id=(block_of(masked(v, d, m)), c),
            device_id_type=MESH,
        )

    def b_own(d, j):
        return pltpu.make_async_copy(
            integrals.at[:, pl.ds(pl.multiple_of(base(d, 0) + j * kb, 128), kb)], slabs.at[d, j, b], own_sem.at[d, j]
        )

    def f_copy(d, j, m):
        block = slabs.at[d, j, block_of(masked(v, d, m))]
        return pltpu.make_async_remote_copy(
            src_ref=block,
            dst_ref=block,
            send_sem=f_send.at[d, j, m],
            recv_sem=f_recv.at[d, j, m],
            device_id=(block_of(flipped(v, [d])), c),
            device_id_type=MESH,
        )

    def f_arrival(d, j, m):
        block = slabs.at[d, j, block_of(flipped(masked(v, d, m), [d]))]
        return pltpu.make_async_remote_copy(
            src_ref=block,
            dst_ref=block,
            send_sem=f_send.at[d, j, m],
            recv_sem=f_recv.at[d, j, m],
            device_id=(block_of(flipped(v, [d])), c),
            device_id_type=MESH,
        )

    def a_copy(d, j, m):
        return pltpu.make_async_remote_copy(
            src_ref=sent.at[d, j, m - 1],
            dst_ref=pairs.at[d, j, spot(v, d)],
            send_sem=a_send.at[d, j, m],
            recv_sem=a_recv.at[d, j, m],
            device_id=(block_of(masked(v, d, m)), c),
            device_id_type=MESH,
        )

    def b_start(j, carry):
        for d in range(3):
            b_own(d, j).start()
            for m in range(1, 4):
                b_copy(d, j, m).start()
        return carry

    lax.fori_loop(0, JB, b_start, 0)

    def add_pairs(slot, m, put):
        back = stage[slot, m, pl.ds(ROWS, ROWS), :].reshape(8, 8, ka)
        back = jnp.swapaxes(back, 0, 1).reshape(ROWS, ka)
        put(stage[slot, m, pl.ds(0, ROWS), :] + back)

    def a_start(j, carry):
        for d in range(3):
            step = j * 3 + d
            slot = step % 2
            for copy in load(step, slot):
                copy.wait()
            if d < 2:
                for copy in load(step + 1, (step + 1) % 2):
                    copy.start()
            else:

                @pl.when(j < JA - 1)
                def _():
                    for copy in load(step + 1, (step + 1) % 2):
                        copy.start()

            for m in range(1, 4):

                def put(value):
                    sent[d, j, m - 1] = value

                add_pairs(slot, m, put)
                a_copy(d, j, m).start()

            def put_own(value):
                pairs[d, j, spot(v, d)] = value

            add_pairs(slot, 0, put_own)
        return carry

    lax.fori_loop(0, JA, a_start, 0)

    def forward(j, carry):
        for d in range(3):
            b_own(d, j).wait()
            f_copy(d, j, 0).start()
            for m in range(1, 4):
                b_copy(d, j, m).wait_recv()
                f_copy(d, j, m).start()
        return carry

    lax.fori_loop(0, JB, forward, 0)

    zeta[...] = jnp.zeros_like(zeta)
    columns[...] = pltpu.roll(singles[...], (N_CD - c) % N_CD * width, 1)[:, :128]

    def multiply(jb, carry):
        for d in range(3):
            for m in range(4):
                f_arrival(d, jb, m).wait_recv()
        for ja in range(JA // JB):
            j = jb * (JA // JB) + ja
            for d in range(3):
                for m in range(1, 4):
                    a_copy(d, j, m).wait_recv()
                left = pairs[d, j].reshape(4 * ROWS, ka)
                right = slabs[d, jb, :, :, pl.ds(ja * ka, ka)].reshape(N_BLK * KA, ka)
                part = product(left, right, ((1,), (1,)))
                for slot in range(4):
                    t = tile_at(v, d, slot)
                    rows = part[slot * ROWS : (slot + 1) * ROWS]
                    zeta[0, t] += rows[:, :128]
                    zeta[1, t] += rows[:, 128:]
        return carry

    lax.fori_loop(0, JB, multiply, 0)

    def to_cd(o):
        peer = (c + o) % N_CD
        return pltpu.make_async_remote_copy(
            src_ref=zeta.at[peer % 2, :, pl.ds(pl.multiple_of(peer // 2 * 8, 8), 8), :],
            dst_ref=parts.at[o],
            send_sem=s1.at[o],
            recv_sem=r1.at[o],
            device_id=(b, peer),
            device_id_type=MESH,
        )

    def to_tile(o):
        peer = (b + o) % N_BLK
        return pltpu.make_async_remote_copy(
            src_ref=summed.at[peer],
            dst_ref=tiles.at[o],
            send_sem=s2.at[o],
            recv_sem=r2.at[o],
            device_id=(peer, c),
            device_id_type=MESH,
        )

    def to_all(o):
        return pltpu.make_async_remote_copy(
            src_ref=whole.at[c % 2, c // 2],
            dst_ref=whole.at[c % 2, c // 2],
            send_sem=s3.at[o],
            recv_sem=r3.at[o],
            device_id=(b, (c + o) % N_CD),
            device_id_type=MESH,
        )

    def from_all(o):
        peer = (c + N_CD - o) % N_CD
        return pltpu.make_async_remote_copy(
            src_ref=whole.at[peer % 2, peer // 2],
            dst_ref=whole.at[peer % 2, peer // 2],
            send_sem=s3.at[o],
            recv_sem=r3.at[o],
            device_id=(b, (c + o) % N_CD),
            device_id_type=MESH,
        )

    for o in range(1, N_CD):
        to_cd(o).start()
    total = zeta[c % 2, :, pl.ds(pl.multiple_of(c // 2 * 8, 8), 8), :]
    for o in range(1, N_CD):
        to_cd(o).wait_recv()
        total = total + parts[o]
    summed[...] = total

    for o in range(1, N_BLK):
        to_tile(o).start()
    mine = summed[b]
    for o in range(1, N_BLK):
        to_tile(o).wait_recv()
        mine = mine + tiles[o]
    whole[c % 2, c // 2] = mine

    for o in range(1, N_CD):
        to_all(o).start()
    for o in range(1, N_CD):
        from_all(o).wait_recv()

    for a in range(2):
        folded[...] = product(whole[a].reshape(ROWS, 128), columns[...], ((1,), (0,)))
        out[a, pl.ds(0, ROWS), :] = folded[...]
        for i in range(8):
            out[a, pl.ds(ROWS + i * 8, 8), :] = folded[pl.ds(i, 8, stride=8), :]

    def drain_b(j, carry):
        for d in range(3):
            f_copy(d, j, 0).wait_send()
            for m in range(1, 4):
                b_copy(d, j, m).wait_send()
                f_copy(d, j, m).wait_send()
        return carry

    def drain_a(j, carry):
        for d in range(3):
            for m in range(1, 4):
                a_copy(d, j, m).wait_send()
        return carry

    lax.fori_loop(0, JB, drain_b, 0)
    lax.fori_loop(0, JA, drain_a, 0)
    for o in range(1, N_CD):
        to_cd(o).wait_send()
        to_all(o).wait_send()
    for o in range(1, N_BLK):
        to_tile(o).wait_send()


def on_device(integrals, tau, singles, doubles):
    depth = integrals.shape[1] // 12
    ka, kb = depth // JA, depth // JB
    width = doubles.shape[2]
    vmem, dma, f32 = pltpu.VMEM, pltpu.SemaphoreType.DMA, jnp.float32
    any_ref, vmem_ref = pl.BlockSpec(memory_space=pl.ANY), pl.BlockSpec(memory_space=vmem)
    folded = pl.pallas_call(
        kernel,
        out_shape=jax.ShapeDtypeStruct((2, 2 * ROWS, 128), f32),
        in_specs=[any_ref, any_ref, vmem_ref],
        out_specs=vmem_ref,
        scratch_shapes=[
            vmem((2, 4, 2 * ROWS, ka), f32),
            vmem((3, JA, 3, ROWS, ka), f32),
            vmem((3, JA, 4, ROWS, ka), f32),
            vmem((3, JB, N_BLK, KA, kb), f32),
            vmem((2, N_BLK, ROWS, 128), f32),
            vmem((N_CD, N_BLK, 8, 128), f32),
            vmem((N_BLK, 8, 128), f32),
            vmem((N_BLK, 8, 128), f32),
            vmem((2, 8, 8, 128), f32),
            vmem((128, 128), f32),
            vmem((ROWS, 128), f32),
            dma((2, 4)), dma((3, JB)),
            dma((3, JA, 4)), dma((3, JA, 4)),
            dma((3, JB, 4)), dma((3, JB, 4)), dma((3, JB, 4)), dma((3, JB, 4)),
            dma((N_CD,)), dma((N_CD,)), dma((N_BLK,)), dma((N_BLK,)), dma((N_CD,)), dma((N_CD,)),
        ],
        compiler_params=pltpu.CompilerParams(
            collective_id=0, has_side_effects=True, vmem_limit_bytes=48 * 2**20
        ),
        cost_estimate=pl.CostEstimate(flops=2 * 3 * 256 * 256 * depth * 3, bytes_accessed=24 * 2**20, transcendentals=0),
    )(tau, integrals, singles)
    return doubles - jnp.transpose(folded, (1, 0, 2))[:, :, :width]


def solution(mesh):
    placed = (P("blk", "cd"), P("blk", "cd"), P(), P("blk", None, "cd"))
    return jax.shard_map(
        on_device, mesh=mesh, in_specs=placed, out_specs=P("blk", None, "cd"), check_vma=False
    )
```

time: 567 us -> 180 us (0.32)
  waiting for transfers between devices: 508 us -> 0 us
  Pallas kernels: 0 us -> 175 us
  matrix products: 43.4 us -> 0 us
  between operations: 13.5 us -> 0.03 us
    all_gather x1 -> x0, waiting for transfers between devices: 372 us -> none  [on_device(): lax.all_gather(integrals, 'blk', axis=0, tiled=True)]
    pallas_call x0 -> x1, Pallas kernels: none -> 175 us  [on_device(): pl.pallas_call(kernel, out_shape=jax.ShapeDtypeStruct((2, 2 * ROWS, 128),...]
    psum x1 -> x0, waiting for transfers between devices: 135 us -> none  [on_device(): zeta = lax.psum(zeta_part, 'cd')]
    dot_general x2 -> x0, matrix products: 43.4 us -> none  [the longest x1 42.1 us: on_device(): lax.dot_general(tau, lax.all_gather(integrals, 'blk', axis=0, tiled=True)...]
  transfers between devices with their start and end apart: 2 -> 0, of which waited for: 2 -> 0; matrix products, arithmetic and copies ran while one was open for 0% -> 0% of each run, Pallas kernels for 0% -> 0%
where the time goes in v1:
time: 180 us; the launch traced here: 179 us
  Pallas kernels  175 us (97%)
  local copies, waits for them, and re-layouts  4.13 us (2%)
    pallas_call x1, Pallas kernels, on_device(): pl.pallas_call(kernel, out_shape=jax.ShapeDtypeStruct((2, 2 * ROWS, 128),...  175 us

profile of v1, /device:TPU:1, one launch (start us, length us, event | category | flops | bytes accessed | tf_op | source)
XLA Modules:
  0.0 179.2 jit_solution(8163360189706256043)
XLA Ops:
  0.0 0.0 copy-start
  0.0 2.3 %copy-done = f32[32,36864]{1,0:T(8,128)S(1)} copy-done((f32[32,36864]{1,0:T(8,128)S(1)}, f32[32,36864]{1,0:T(8,128)}, u32[]{:S(2)}) %copy-start) | copy-done | bytes 4718616
  2.3 0.0 copy-start.1
  2.3 1.0 copy-done.1
  3.3 0.0 copy-start.2
  3.3 175.1 %shard_map.46 = f32[2,128,128]{2,1,0:T(8,128)S(1)} custom-call(f32[128,36864]{1,0:T(8,128)} %tau.1, f32[32,36864]{1,0:T(8,128)S(1)} %copy-done, f32[128,768]{1,0:T(8,128)S(1)} %copy-done.1), custom_call_target="tpu_custom_call" | custom-call | flops 3623878656 | bytes 25165824 | tf_op jit(solution)/shard_map/pallas_call | solution.py:326
  178.4 0.0 copy-done.2
  178.4 0.1 copy.7
  178.5 0.7 copy.8
  (1 shorter events, 0.0 us)
Async XLA Ops:
  0.0 2.3 %copy-start = (f32[32,36864]{1,0:T(8,128)S(1)}, f32[32,36864]{1,0:T(8,128)}, u32[]{:S(2)}) copy-start(f32[32,36864]{1,0:T(8,128)} %integrals.1) | copy-start | bytes 14155780
  2.3 1.0 copy-start.1
  3.3 175.1 %copy-start.2 = (f32[128,2,48]{0,2,1:T(8,128)S(1)}, f32[128,2,48]{0,2,1:T(8,128)}, u32[]{:S(2)}) copy-start(f32[128,2,48]{0,2,1:T(8,128)} %param.7) | copy-start | bytes 147460

commit v2 on v0

v2 whole, which is shorter than its diff:
```python
import jax
import jax.numpy as jnp
from jax import lax
from jax.experimental import pallas as pl
from jax.experimental.pallas import tpu as pltpu
from jax.sharding import PartitionSpec as P

MESH = pl.DeviceIdType.MESH
N_BLK, N_CD = 8, 16
ROWS, KA = 64, 32
LATE = 8
EARLY = ROWS - LATE
STEPS = 6
LATE_STEPS = 3
PER_LATE = STEPS // LATE_STEPS
OTHERS = ((1, 2), (0, 2), (0, 1))
ORDER = ((0, 1), (1, 2), (2, 1), (1, 1), (2, 2), (0, 2), (0, 3), (2, 3), (1, 3))


def corner(b):
    x = b % 4
    return (((x + 1) // 2) % 2, x // 2, b // 4)


def block_of(v):
    return v[2] * 4 + v[1] * 2 + (v[0] + v[1]) % 2


def flipped(v, dims):
    return tuple((e + 1) % 2 if at in dims else e for at, e in enumerate(v))


def masked(v, d, m):
    return flipped(v, [o for bit, o in enumerate(OTHERS[d]) if (m >> bit) & 1])


def spot(v, d):
    return v[OTHERS[d][0]] + 2 * v[OTHERS[d][1]]


def tile_at(v, d, slot):
    new = list(v)
    new[OTHERS[d][0]] = slot % 2
    new[OTHERS[d][1]] = slot // 2
    return block_of(new)


def halves(x):
    high = x.astype(jnp.bfloat16)
    return high, (x - high.astype(jnp.float32)).astype(jnp.bfloat16)


def product(a, b):
    def dot(l, r):
        return lax.dot_general(l, r, (((1,), (1,)), ((), ())), preferred_element_type=jnp.float32)

    return dot(a[0], b[0]) + (dot(a[0], b[1]) + dot(a[1], b[0]))


def arrive(ref, sem):
    pltpu.make_async_copy(ref, ref, sem).wait()


def kernel(
    tau, integrals, singles, out,
    stage, early, late, slabs, high, low, zeta, zeta_late,
    parts, summed, pieces, whole, tiles, spreads, factors, columns, spread,
    load_sem, own_sem, factor_sem, a_send, early_recv, late_recv, b_send, b_recv, f_recv, t_send, t_recv,
):
    b, c = lax.axis_index("blk"), lax.axis_index("cd")
    v = corner(b)
    depth = integrals.shape[1] // 12
    ka = depth // STEPS
    width = singles.shape[1] // N_CD
    zh, yc = c // 2 % 2, c // 4 * 2 + c % 2

    def cd_of(zh, yc):
        return yc // 2 * 4 + zh * 2 + yc % 2

    def span(d, j, m):
        return pl.ds(pl.multiple_of((d * 4 + spot(masked(v, d, m), d)) * depth + j * ka, 128), ka)

    def send(src, dst, sent, got, blk, cd):
        pltpu.make_async_remote_copy(
            src_ref=src, dst_ref=dst, send_sem=sent, recv_sem=got, device_id=(blk, cd), device_id_type=MESH
        ).start()

    def load_start(j, carry):
        for d in range(3):
            for m in range(4):
                pltpu.make_async_copy(tau.at[:, span(d, j, m)], stage.at[j, d, m], load_sem.at[j]).start()
        return carry

    lax.fori_loop(0, STEPS, load_start, 0)
    factor_copy = pltpu.make_async_copy(singles, factors, factor_sem)
    factor_copy.start()

    def own_start(j, carry):
        for d in range(3):
            pltpu.make_async_copy(integrals.at[:, span(d, j, 0)], slabs.at[j, d, b], own_sem).start()
        return carry

    lax.fori_loop(0, STEPS, own_start, 0)

    barrier = pltpu.get_barrier_semaphore()
    for o in range(1, N_BLK):
        pl.semaphore_signal(barrier, inc=1, device_id=((b + o) % N_BLK, c), device_id_type=MESH)
    for o in range(1, N_CD):
        pl.semaphore_signal(barrier, inc=1, device_id=(b, (c + o) % N_CD), device_id_type=MESH)
    pl.semaphore_wait(barrier, N_BLK + N_CD - 2)

    def b_start(j, carry):
        for d, m in ORDER:
            send(
                integrals.at[:, span(d, j, m)], slabs.at[j, d, b], b_send, b_recv.at[j], block_of(masked(v, d, m)), c
            )
        return carry

    lax.fori_loop(0, STEPS, b_start, 0)

    def pair_sums(j, d, m):
        back = stage[j, d, m, pl.ds(ROWS, ROWS), :].reshape(8, 8, ka)
        back = jnp.swapaxes(back, 0, 1).reshape(ROWS, ka)
        return stage[j, d, m, pl.ds(0, ROWS), :] + back

    def early_start(j, carry):
        arrive(stage.at[j], load_sem.at[j])
        for d, m in ORDER:
            stage[j, d, m, pl.ds(0, ROWS), :] = pair_sums(j, d, m)
            send(
                stage.at[j, d, m, pl.ds(0, EARLY), :], early.at[j, d, spot(v, d)],
                a_send, early_recv.at[j, d], block_of(masked(v, d, m)), c,
            )
        for d in range(3):
            sums = pair_sums(j, d, 0)
            early[j, d, spot(v, d)] = sums[:EARLY]
            late[j, d, spot(v, d)] = sums[EARLY:]
        return carry

    lax.fori_loop(0, STEPS, early_start, 0)

    arrive(slabs.at[:, :, 0], own_sem)

    def forward(j, carry):
        arrive(slabs.at[j, :, pl.ds(0, 3)], b_recv.at[j])
        for m in range(4):
            for d in range(3):
                block = slabs.at[j, d, block_of(masked(v, d, m))]
                send(block, block, b_send, f_recv.at[j], block_of(flipped(v, [d])), c)
        return carry

    lax.fori_loop(0, STEPS, forward, 0)

    def late_start(n, carry):
        steps = pl.ds(n * PER_LATE, PER_LATE)
        for d, m in ORDER:
            send(
                stage.at[steps, d, m, pl.ds(EARLY, LATE), :], late.at[steps, d, spot(v, d)],
                a_send, late_recv.at[n, d], block_of(masked(v, d, m)), c,
            )
        return carry

    lax.fori_loop(0, LATE_STEPS, late_start, 0)

    zeta[...] = jnp.zeros_like(zeta)
    zeta_late[...] = jnp.zeros_like(zeta_late)
    factor_copy.wait()
    columns[...] = pltpu.roll(factors[...], (N_CD - c) % N_CD * width, 1)[:, :128].T

    def multiply_early(j, carry):
        arrive(slabs.at[j, :, pl.ds(0, 4)], f_recv.at[j])
        for d in range(3):
            right = halves(slabs[j, d].reshape(N_BLK * KA, ka))
            high[j, d], low[j, d] = right
            arrive(early.at[j, d, pl.ds(0, 3)], early_recv.at[j, d])
            part = product(halves(early[j, d].reshape(4 * EARLY, ka)), right)
            for slot in range(4):
                t = tile_at(v, d, slot)
                rows = part[slot * EARLY : (slot + 1) * EARLY]
                for a in range(2):
                    zeta[t, a, pl.ds(0, EARLY // 8)] += rows[:, a * 128 : (a + 1) * 128].reshape(EARLY // 8, 8, 128)
        return carry

    lax.fori_loop(0, STEPS, multiply_early, 0)

    for o in range(1, 8):
        peer = (yc + o) % 8
        share = zeta.at[:, peer // 4, pl.ds(peer % 4 * 2, 2)]
        send(share, parts.at[o], t_send.at[0], t_recv.at[0], b, cd_of(zh, peer))

    def multiply_late(n, carry):
        for d in range(3):
            arrive(late.at[pl.ds(0, PER_LATE), d, pl.ds(0, 3)], late_recv.at[n, d])
            for s in range(PER_LATE):
                j = n * PER_LATE + s
                part = product(halves(late[j, d].reshape(4 * LATE, ka)), (high[j, d], low[j, d]))
                for slot in range(4):
                    t = tile_at(v, d, slot)
                    rows = part[slot * LATE : (slot + 1) * LATE]
                    for a in range(2):
                        zeta_late[t, a] += rows[:, a * 128 : (a + 1) * 128]
        return carry

    lax.fori_loop(0, LATE_STEPS - 1, multiply_late, 0)

    arrive(parts.at[pl.ds(1, 7)], t_recv.at[0])
    total = zeta[:, yc // 4, pl.ds(yc % 4 * 2, 2)]
    for o in range(1, 8):
        total = total + parts[o]
    summed[...] = total
    for o in range(1, N_BLK):
        peer = (b + o) % N_BLK
        send(summed.at[peer], pieces.at[o], t_send.at[1], t_recv.at[1], peer, c)

    multiply_late(LATE_STEPS - 1, 0)

    for o in range(1, N_BLK):
        peer = (b + o) % N_BLK
        send(zeta_late.at[peer], tiles.at[o], t_send.at[3], t_recv.at[3], peer, c)

    arrive(pieces.at[pl.ds(1, 7)], t_recv.at[1])
    mine = summed[b]
    for o in range(1, N_BLK):
        mine = mine + pieces[o]
    whole[c] = mine
    for o in range(1, N_CD):
        send(whole.at[c], whole.at[c], t_send.at[2], t_recv.at[2], b, (c + o) % N_CD)

    arrive(tiles.at[pl.ds(1, 7)], t_recv.at[3])
    last = zeta_late[b]
    for o in range(1, N_BLK):
        last = last + tiles[o]
    spreads[c] = last
    for o in range(1, N_CD):
        send(spreads.at[c], spreads.at[c], t_send.at[4], t_recv.at[4], b, (c + o) % N_CD)

    arrive(whole.at[pl.ds(1, 15)], t_recv.at[2])
    for a in range(2):
        for i in range(7):
            rows = whole[cd_of(0, a * 4 + i // 2), i % 2] + whole[cd_of(1, a * 4 + i // 2), i % 2]
            spread[a, pl.ds(i * 8, 8), :] = rows
            spread[a, pl.ds(ROWS + i, 8, stride=8), :] = rows

    arrive(spreads.at[pl.ds(1, 15)], t_recv.at[4])
    last = spreads[0]
    for o in range(1, N_CD):
        last = last + spreads[o]
    left = halves(columns[pl.ds(0, width), :])
    for a in range(2):
        spread[a, pl.ds(EARLY, 8), :] = last[a]
        spread[a, pl.ds(ROWS + 7, 8, stride=8), :] = last[a]
        out[a] = product(left, halves(spread[a]))

    arrive(slabs.at[:, :, pl.ds(0, 7)], b_send)
    arrive(early.at[:, :, pl.ds(0, 3)], a_send)
    arrive(late.at[:, :, pl.ds(0, 3)], a_send)
    arrive(parts.at[pl.ds(1, 7)], t_send.at[0])
    arrive(pieces.at[pl.ds(1, 7)], t_send.at[1])
    arrive(whole.at[pl.ds(1, 15)], t_send.at[2])
    arrive(tiles.at[pl.ds(1, 7)], t_send.at[3])
    arrive(spreads.at[pl.ds(1, 15)], t_send.at[4])


def on_device(integrals, tau, singles, doubles):
    depth = integrals.shape[1] // 12
    ka = depth // STEPS
    width = doubles.shape[2]
    vmem, dma, f32 = pltpu.VMEM, pltpu.SemaphoreType.DMA, jnp.float32
    any_ref, vmem_ref = pl.BlockSpec(memory_space=pl.ANY), pl.BlockSpec(memory_space=vmem)
    folded = pl.pallas_call(
        kernel,
        out_shape=jax.ShapeDtypeStruct((2, width, 2 * ROWS), f32),
        in_specs=[any_ref, any_ref, any_ref],
        out_specs=vmem_ref,
        scratch_shapes=[
            vmem((STEPS, 3, 4, 2 * ROWS, ka), f32),
            vmem((STEPS, 3, 4, EARLY, ka), f32),
            vmem((STEPS, 3, 4, LATE, ka), f32),
            vmem((STEPS, 3, N_BLK, KA, ka), f32),
            vmem((STEPS, 3, N_BLK * KA, ka), jnp.bfloat16),
            vmem((STEPS, 3, N_BLK * KA, ka), jnp.bfloat16),
            vmem((N_BLK, 2, 8, 8, 128), f32),
            vmem((N_BLK, 2, LATE, 128), f32),
            vmem((8, N_BLK, 2, 8, 128), f32),
            vmem((N_BLK, 2, 8, 128), f32),
            vmem((N_BLK, 2, 8, 128), f32),
            vmem((N_CD, 2, 8, 128), f32),
            vmem((N_BLK, 2, LATE, 128), f32),
            vmem((N_CD, 2, LATE, 128), f32),
            vmem(singles.shape, f32),
            vmem((128, 128), f32),
            vmem((2, 2 * ROWS, 128), f32),
            dma((STEPS,)), dma(()), dma(()),
            dma(()), dma((STEPS, 3)), dma((LATE_STEPS, 3)),
            dma(()), dma((STEPS,)), dma((STEPS,)),
            dma((5,)), dma((5,)),
        ],
        compiler_params=pltpu.CompilerParams(
            collective_id=0, has_side_effects=True, vmem_limit_bytes=60 * 2**20
        ),
        cost_estimate=pl.CostEstimate(flops=2 * 3 * 256 * 256 * depth * 3, bytes_accessed=24 * 2**20, transcendentals=0),
    )(tau, integrals, singles)
    return doubles - jnp.transpose(folded, (2, 0, 1))


def solution(mesh):
    placed = (P("blk", "cd"), P("blk", "cd"), P(), P("blk", None, "cd"))
    return jax.shard_map(
        on_device, mesh=mesh, in_specs=placed, out_specs=P("blk", None, "cd"), check_vma=False
    )
```

time: 567 us -> 164 us (0.29)
  waiting for transfers between devices: 508 us -> 0 us
  Pallas kernels: 0 us -> 162 us
  matrix products: 43.4 us -> 0 us
  between operations: 13.5 us -> 0.02 us
    all_gather x1 -> x0, waiting for transfers between devices: 372 us -> none  [on_device(): lax.all_gather(integrals, 'blk', axis=0, tiled=True)]
    pallas_call x0 -> x1, Pallas kernels: none -> 162 us  [on_device(): pl.pallas_call(kernel, out_shape=jax.ShapeDtypeStruct((2, width, 2 * ROWS...]
    psum x1 -> x0, waiting for transfers between devices: 135 us -> none  [on_device(): zeta = lax.psum(zeta_part, 'cd')]
    dot_general x2 -> x0, matrix products: 43.4 us -> none  [the longest x1 42.1 us: on_device(): lax.dot_general(tau, lax.all_gather(integrals, 'blk', axis=0, tiled=True)...]
  transfers between devices with their start and end apart: 2 -> 0, of which waited for: 2 -> 0; matrix products, arithmetic and copies ran while one was open for 0% -> 0% of each run, Pallas kernels for 0% -> 0%
where the time goes in v2:
time: 164 us
  Pallas kernels  162 us (99%)
    pallas_call x1, Pallas kernels, on_device(): pl.pallas_call(kernel, out_shape=jax.ShapeDtypeStruct((2, width, 2 * ROWS...  162 us

profile of v2, /device:TPU:1, one launch (start us, length us, event | category | flops | bytes accessed | tf_op | source)
XLA Modules:
  0.0 163.5 jit_solution(11073625093364498355)
XLA Ops:
  0.0 0.0 copy-start
  0.0 162.1 %shard_map.46 = f32[2,48,128]{2,1,0:T(8,128)} custom-call(f32[128,36864]{1,0:T(8,128)} %tau.1, f32[32,36864]{1,0:T(8,128)} %integrals.1, f32[128,768]{1,0:T(8,128)} %singles.1), custom_call_target="tpu_custom_call" | custom-call | flops 3623878656 | bytes 25165824 | tf_op jit(solution)/shard_map/pallas_call | solution.py:270
  162.1 0.0 copy-done
  162.1 1.4 bitcast_subtract_fusion
Async XLA Ops:
  0.0 162.1 %copy-start = (f32[128,2,48]{0,2,1:T(8,128)S(1)}, f32[128,2,48]{0,2,1:T(8,128)}, u32[]{:S(2)}) copy-start(f32[128,2,48]{0,2,1:T(8,128)} %param.7) | copy-start | bytes 147460

commit v3 on v2

--- a/solution.py
+++ b/solution.py
@@ -8,12 +8,13 @@
 MESH = pl.DeviceIdType.MESH
 N_BLK, N_CD = 8, 16
 ROWS, KA = 64, 32
-LATE = 8
-EARLY = ROWS - LATE
+LATE, N_LATE = 8, 2
+EARLY = ROWS - LATE * N_LATE
 STEPS = 6
-LATE_STEPS = 3
-PER_LATE = STEPS // LATE_STEPS
+LATE_STEPS = (6, 6)
 OTHERS = ((1, 2), (0, 2), (0, 1))
+FAR_CD = (10, 11, 6, 7, 14, 15, 8, 9, 2, 3, 4, 5, 12, 13, 1)
+FAR_BLK = (6, 2, 5, 7, 4, 1, 3)
 ORDER = ((0, 1), (1, 2), (2, 1), (1, 1), (2, 2), (0, 2), (0, 3), (2, 3), (1, 3))
 
 
@@ -50,10 +51,14 @@
     return high, (x - high.astype(jnp.float32)).astype(jnp.bfloat16)
 
 
-def product(a, b):
+def product(a, b, stacked=False):
     def dot(l, r):
         return lax.dot_general(l, r, (((1,), (1,)), ((), ())), preferred_element_type=jnp.float32)
 
+    if stacked:
+        both = dot(jnp.concatenate(a), b[0])
+        n = a[0].shape[0]
+        return both[:n] + (dot(a[0], b[1]) + both[n:])
     return dot(a[0], b[0]) + (dot(a[0], b[1]) + dot(a[1], b[0]))
 
 
@@ -77,6 +82,12 @@
     def cd_of(zh, yc):
         return yc // 2 * 4 + zh * 2 + yc % 2
 
+    def cd_at(o):
+        return (c // 4 + o // 4) % 4 * 4 + (c // 2 + o // 2) % 2 * 2 + (c + o) % 2
+
+    def blk_at(o):
+        return (b // 4 + o // 4) % 2 * 4 + (b + o) % 4
+
     def span(d, j, m):
         return pl.ds(pl.multiple_of((d * 4 + spot(masked(v, d, m), d)) * depth + j * ka, 128), ka)
 
@@ -85,6 +96,12 @@
             src_ref=src, dst_ref=dst, send_sem=sent, recv_sem=got, device_id=(blk, cd), device_id_type=MESH
         ).start()
 
+    barrier = pltpu.get_barrier_semaphore()
+    for o in FAR_CD:
+        pl.semaphore_signal(barrier, inc=1, device_id=(b, cd_at(o)), device_id_type=MESH)
+    for o in FAR_BLK:
+        pl.semaphore_signal(barrier, inc=1, device_id=(blk_at(o), c), device_id_type=MESH)
+
     def load_start(j, carry):
         for d in range(3):
             for m in range(4):
@@ -102,11 +119,6 @@
 
     lax.fori_loop(0, STEPS, own_start, 0)
 
-    barrier = pltpu.get_barrier_semaphore()
-    for o in range(1, N_BLK):
-        pl.semaphore_signal(barrier, inc=1, device_id=((b + o) % N_BLK, c), device_id_type=MESH)
-    for o in range(1, N_CD):
-        pl.semaphore_signal(barrier, inc=1, device_id=(b, (c + o) % N_CD), device_id_type=MESH)
     pl.semaphore_wait(barrier, N_BLK + N_CD - 2)
 
     def b_start(j, carry):
@@ -134,7 +146,8 @@
         for d in range(3):
             sums = pair_sums(j, d, 0)
             early[j, d, spot(v, d)] = sums[:EARLY]
-            late[j, d, spot(v, d)] = sums[EARLY:]
+            for g in range(N_LATE):
+                late[g, j, d, spot(v, d)] = sums[EARLY + g * LATE : EARLY + (g + 1) * LATE]
         return carry
 
     lax.fori_loop(0, STEPS, early_start, 0)
@@ -151,16 +164,22 @@
 
     lax.fori_loop(0, STEPS, forward, 0)
 
-    def late_start(n, carry):
-        steps = pl.ds(n * PER_LATE, PER_LATE)
-        for d, m in ORDER:
-            send(
-                stage.at[steps, d, m, pl.ds(EARLY, LATE), :], late.at[steps, d, spot(v, d)],
-                a_send, late_recv.at[n, d], block_of(masked(v, d, m)), c,
-            )
-        return carry
-
-    lax.fori_loop(0, LATE_STEPS, late_start, 0)
+    def late_start(g):
+        per = STEPS // LATE_STEPS[g]
+
+        def start(n, carry):
+            steps = pl.ds(n * per, per)
+            for d, m in ORDER:
+                send(
+                    stage.at[steps, d, m, pl.ds(EARLY + g * LATE, LATE), :], late.at[g, steps, d, spot(v, d)],
+                    a_send, late_recv.at[g, n, d], block_of(masked(v, d, m)), c,
+                )
+            return carry
+
+        lax.fori_loop(0, LATE_STEPS[g], start, 0)
+
+    for g in range(N_LATE):
+        late_start(g)
 
     zeta[...] = jnp.zeros_like(zeta)
     zeta_late[...] = jnp.zeros_like(zeta_late)
@@ -183,82 +202,104 @@
 
     lax.fori_loop(0, STEPS, multiply_early, 0)
 
-    for o in range(1, 8):
-        peer = (yc + o) % 8
+    for o in (4, 5, 2, 3, 6, 7, 1):
+        peer = (yc // 2 + o // 2) % 4 * 2 + (yc + o) % 2
         share = zeta.at[:, peer // 4, pl.ds(peer % 4 * 2, 2)]
         send(share, parts.at[o], t_send.at[0], t_recv.at[0], b, cd_of(zh, peer))
 
-    def multiply_late(n, carry):
-        for d in range(3):
-            arrive(late.at[pl.ds(0, PER_LATE), d, pl.ds(0, 3)], late_recv.at[n, d])
-            for s in range(PER_LATE):
-                j = n * PER_LATE + s
-                part = product(halves(late[j, d].reshape(4 * LATE, ka)), (high[j, d], low[j, d]))
-                for slot in range(4):
-                    t = tile_at(v, d, slot)
-                    rows = part[slot * LATE : (slot + 1) * LATE]
-                    for a in range(2):
-                        zeta_late[t, a] += rows[:, a * 128 : (a + 1) * 128]
-        return carry
-
-    lax.fori_loop(0, LATE_STEPS - 1, multiply_late, 0)
+    def multiply_late(g, first, end):
+        per = STEPS // LATE_STEPS[g]
+
+        def multiply(n, carry):
+            for d in range(3):
+                arrive(late.at[g, pl.ds(0, per), d, pl.ds(0, 3)], late_recv.at[g, n, d])
+                for s in range(per):
+                    j = n * per + s
+                    part = product(halves(late[g, j, d].reshape(4 * LATE, ka)), (high[j, d], low[j, d]), True)
+                    for slot in range(4):
+                        t = tile_at(v, d, slot)
+                        rows = part[slot * LATE : (slot + 1) * LATE]
+                        for a in range(2):
+                            zeta_late[g, t, a] += rows[:, a * 128 : (a + 1) * 128]
+            return carry
+
+        lax.fori_loop(first, end, multiply, 0)
+
+    def late_to_tiles(g):
+        for o in FAR_BLK:
+            peer = blk_at(o)
+            send(zeta_late.at[g, peer], tiles.at[g, o], t_send.at[3 + g], t_recv.at[3 + g], peer, c)
+
+    def late_to_all(g):
+        arrive(tiles.at[g, pl.ds(1, 7)], t_recv.at[3 + g])
+        last = zeta_late[g, b]
+        for o in range(1, N_BLK):
+            last = last + tiles[g, o]
+        spreads[g, c] = last
+        for o in FAR_CD:
+            send(
+                spreads.at[g, c], spreads.at[g, c],
+                t_send.at[3 + N_LATE + g], t_recv.at[3 + N_LATE + g], b, cd_at(o),
+            )
+
+    def late_rows(g):
+        arrive(spreads.at[g, pl.ds(1, 15)], t_recv.at[3 + N_LATE + g])
+        last = spreads[g, 0]
+        for o in range(1, N_CD):
+            last = last + spreads[g, o]
+        at = EARLY // 8 + g
+        for a in range(2):
+            spread[a, pl.ds(at * 8, 8), :] = last[a]
+            spread[a, pl.ds(ROWS + at, 8, stride=8), :] = last[a]
+
+    multiply_late(0, 0, LATE_STEPS[0])
+    late_to_tiles(0)
 
     arrive(parts.at[pl.ds(1, 7)], t_recv.at[0])
     total = zeta[:, yc // 4, pl.ds(yc % 4 * 2, 2)]
     for o in range(1, 8):
         total = total + parts[o]
     summed[...] = total
-    for o in range(1, N_BLK):
-        peer = (b + o) % N_BLK
+    for o in FAR_BLK:
+        peer = blk_at(o)
         send(summed.at[peer], pieces.at[o], t_send.at[1], t_recv.at[1], peer, c)
 
-    multiply_late(LATE_STEPS - 1, 0)
-
-    for o in range(1, N_BLK):
-        peer = (b + o) % N_BLK
-        send(zeta_late.at[peer], tiles.at[o], t_send.at[3], t_recv.at[3], peer, c)
+    multiply_late(1, 0, LATE_STEPS[1] - 1)
+    late_to_all(0)
+    multiply_late(1, LATE_STEPS[1] - 1, LATE_STEPS[1])
+    late_to_tiles(1)
 
     arrive(pieces.at[pl.ds(1, 7)], t_recv.at[1])
     mine = summed[b]
     for o in range(1, N_BLK):
         mine = mine + pieces[o]
     whole[c] = mine
-    for o in range(1, N_CD):
-        send(whole.at[c], whole.at[c], t_send.at[2], t_recv.at[2], b, (c + o) % N_CD)
-
-    arrive(tiles.at[pl.ds(1, 7)], t_recv.at[3])
-    last = zeta_late[b]
-    for o in range(1, N_BLK):
-        last = last + tiles[o]
-    spreads[c] = last
-    for o in range(1, N_CD):
-        send(spreads.at[c], spreads.at[c], t_send.at[4], t_recv.at[4], b, (c + o) % N_CD)
-
+    for o in FAR_CD:
+        send(whole.at[c], whole.at[c], t_send.at[2], t_recv.at[2], b, cd_at(o))
+
+    late_to_all(1)
     arrive(whole.at[pl.ds(1, 15)], t_recv.at[2])
     for a in range(2):
-        for i in range(7):
+        for i in range(EARLY // 8):
             rows = whole[cd_of(0, a * 4 + i // 2), i % 2] + whole[cd_of(1, a * 4 + i // 2), i % 2]
             spread[a, pl.ds(i * 8, 8), :] = rows
             spread[a, pl.ds(ROWS + i, 8, stride=8), :] = rows
 
-    arrive(spreads.at[pl.ds(1, 15)], t_recv.at[4])
-    last = spreads[0]
-    for o in range(1, N_CD):
-        last = last + spreads[o]
-    left = halves(columns[pl.ds(0, width), :])
-    for a in range(2):
-        spread[a, pl.ds(EARLY, 8), :] = last[a]
-        spread[a, pl.ds(ROWS + 7, 8, stride=8), :] = last[a]
-        out[a] = product(left, halves(spread[a]))
-
+    late_rows(0)
     arrive(slabs.at[:, :, pl.ds(0, 7)], b_send)
     arrive(early.at[:, :, pl.ds(0, 3)], a_send)
-    arrive(late.at[:, :, pl.ds(0, 3)], a_send)
+    arrive(late.at[:, :, :, pl.ds(0, 3)], a_send)
     arrive(parts.at[pl.ds(1, 7)], t_send.at[0])
     arrive(pieces.at[pl.ds(1, 7)], t_send.at[1])
+    left = halves(columns[pl.ds(0, width), :])
+    late_rows(1)
+    for a in range(2):
+        out[a] = product(left, halves(spread[a]))
+
     arrive(whole.at[pl.ds(1, 15)], t_send.at[2])
-    arrive(tiles.at[pl.ds(1, 7)], t_send.at[3])
-    arrive(spreads.at[pl.ds(1, 15)], t_send.at[4])
+    for g in range(N_LATE):
+        arrive(tiles.at[g, pl.ds(1, 7)], t_send.at[3 + g])
+        arrive(spreads.at[g, pl.ds(1, 15)], t_send.at[3 + N_LATE + g])
 
 
 def on_device(integrals, tau, singles, doubles):
@@ -275,25 +316,25 @@
         scratch_shapes=[
             vmem((STEPS, 3, 4, 2 * ROWS, ka), f32),
             vmem((STEPS, 3, 4, EARLY, ka), f32),
-            vmem((STEPS, 3, 4, LATE, ka), f32),
+            vmem((N_LATE, STEPS, 3, 4, LATE, ka), f32),
             vmem((STEPS, 3, N_BLK, KA, ka), f32),
             vmem((STEPS, 3, N_BLK * KA, ka), jnp.bfloat16),
             vmem((STEPS, 3, N_BLK * KA, ka), jnp.bfloat16),
             vmem((N_BLK, 2, 8, 8, 128), f32),
-            vmem((N_BLK, 2, LATE, 128), f32),
+            vmem((N_LATE, N_BLK, 2, LATE, 128), f32),
             vmem((8, N_BLK, 2, 8, 128), f32),
             vmem((N_BLK, 2, 8, 128), f32),
             vmem((N_BLK, 2, 8, 128), f32),
             vmem((N_CD, 2, 8, 128), f32),
-            vmem((N_BLK, 2, LATE, 128), f32),
-            vmem((N_CD, 2, LATE, 128), f32),
+            vmem((N_LATE, N_BLK, 2, LATE, 128), f32),
+            vmem((N_LATE, N_CD, 2, LATE, 128), f32),
             vmem(singles.shape, f32),
             vmem((128, 128), f32),
             vmem((2, 2 * ROWS, 128), f32),
             dma((STEPS,)), dma(()), dma(()),
-            dma(()), dma((STEPS, 3)), dma((LATE_STEPS, 3)),
+            dma(()), dma((STEPS, 3)), dma((N_LATE, max(LATE_STEPS), 3)),
             dma(()), dma((STEPS,)), dma((STEPS,)),
-            dma((5,)), dma((5,)),
+            dma((3 + 2 * N_LATE,)), dma((3 + 2 * N_LATE,)),
         ],
         compiler_params=pltpu.CompilerParams(
             collective_id=0, has_side_effects=True, vmem_limit_bytes=60 * 2**20

time: 164 us -> 161 us (0.982)
  Pallas kernels: 162 us -> 159 us
    pallas_call x1, Pallas kernels: 162 us -> 159 us  [on_device(): pl.pallas_call(kernel, out_shape=jax.ShapeDtypeStruct((2, width, 2 * ROWS...]
where the time goes in v3:
time: 161 us
  Pallas kernels  159 us (99%)
    pallas_call x1, Pallas kernels, on_device(): pl.pallas_call(kernel, out_shape=jax.ShapeDtypeStruct((2, width, 2 * ROWS...  159 us

profile of v3, /device:TPU:1, one launch (start us, length us, event | category | flops | bytes accessed | tf_op | source)
XLA Modules:
  0.0 160.9 jit_solution(14321988323286341773)
XLA Ops:
  0.0 0.0 copy-start
  0.0 159.5 %shard_map.46 = f32[2,48,128]{2,1,0:T(8,128)} custom-call(f32[128,36864]{1,0:T(8,128)} %tau.1, f32[32,36864]{1,0:T(8,128)} %integrals.1, f32[128,768]{1,0:T(8,128)} %singles.1), custom_call_target="tpu_custom_call" | custom-call | flops 3623878656 | bytes 25165824 | tf_op jit(solution)/shard_map/pallas_call | solution.py:311
  159.5 0.0 copy-done
  159.5 1.4 bitcast_subtract_fusion
Async XLA Ops:
  0.0 159.5 %copy-start = (f32[128,2,48]{0,2,1:T(8,128)S(1)}, f32[128,2,48]{0,2,1:T(8,128)}, u32[]{:S(2)}) copy-start(f32[128,2,48]{0,2,1:T(8,128)} %param.7) | copy-start | bytes 147460

commit v4 on v3

--- a/solution.py
+++ b/solution.py
@@ -10,11 +10,12 @@
 ROWS, KA = 64, 32
 LATE, N_LATE = 8, 2
 EARLY = ROWS - LATE * N_LATE
-STEPS = 6
+STEPS = 12
 LATE_STEPS = (6, 6)
 OTHERS = ((1, 2), (0, 2), (0, 1))
 FAR_CD = (10, 11, 6, 7, 14, 15, 8, 9, 2, 3, 4, 5, 12, 13, 1)
 FAR_BLK = (6, 2, 5, 7, 4, 1, 3)
+FAR_YC = (4, 5, 2, 3, 6, 7, 1)
 ORDER = ((0, 1), (1, 2), (2, 1), (1, 1), (2, 2), (0, 2), (0, 3), (2, 3), (1, 3))
 
 
@@ -164,7 +165,7 @@
 
     lax.fori_loop(0, STEPS, forward, 0)
 
-    def late_start(g):
+    def late_start(g, first, end):
         per = STEPS // LATE_STEPS[g]
 
         def start(n, carry):
@@ -176,10 +177,7 @@
                 )
             return carry
 
-        lax.fori_loop(0, LATE_STEPS[g], start, 0)
-
-    for g in range(N_LATE):
-        late_start(g)
+        lax.fori_loop(first, end, start, 0)
 
     zeta[...] = jnp.zeros_like(zeta)
     zeta_late[...] = jnp.zeros_like(zeta_late)
@@ -200,27 +198,24 @@
                     zeta[t, a, pl.ds(0, EARLY // 8)] += rows[:, a * 128 : (a + 1) * 128].reshape(EARLY // 8, 8, 128)
         return carry
 
-    lax.fori_loop(0, STEPS, multiply_early, 0)
-
-    for o in (4, 5, 2, 3, 6, 7, 1):
-        peer = (yc // 2 + o // 2) % 4 * 2 + (yc + o) % 2
-        share = zeta.at[:, peer // 4, pl.ds(peer % 4 * 2, 2)]
-        send(share, parts.at[o], t_send.at[0], t_recv.at[0], b, cd_of(zh, peer))
-
     def multiply_late(g, first, end):
         per = STEPS // LATE_STEPS[g]
 
         def multiply(n, carry):
             for d in range(3):
                 arrive(late.at[g, pl.ds(0, per), d, pl.ds(0, 3)], late_recv.at[g, n, d])
+            found = []
+            for d in range(3):
                 for s in range(per):
                     j = n * per + s
-                    part = product(halves(late[g, j, d].reshape(4 * LATE, ka)), (high[j, d], low[j, d]), True)
-                    for slot in range(4):
-                        t = tile_at(v, d, slot)
-                        rows = part[slot * LATE : (slot + 1) * LATE]
-                        for a in range(2):
-                            zeta_late[g, t, a] += rows[:, a * 128 : (a + 1) * 128]
+                    left = halves(late[g, j, d].reshape(4 * LATE, ka))
+                    found.append((d, product(left, (high[j, d], low[j, d]), True)))
+            for d, part in found:
+                for slot in range(4):
+                    t = tile_at(v, d, slot)
+                    rows = part[slot * LATE : (slot + 1) * LATE]
+                    for a in range(2):
+                        zeta_late[g, t, a] += rows[:, a * 128 : (a + 1) * 128]
             return carry
 
         lax.fori_loop(first, end, multiply, 0)
@@ -252,9 +247,19 @@
             spread[a, pl.ds(at * 8, 8), :] = last[a]
             spread[a, pl.ds(ROWS + at, 8, stride=8), :] = last[a]
 
-    multiply_late(0, 0, LATE_STEPS[0])
+    lax.fori_loop(0, 8, multiply_early, 0)
+    late_start(0, 0, 3)
+    lax.fori_loop(8, 12, multiply_early, 0)
+    for o in FAR_YC:
+        peer = (yc // 2 + o // 2) % 4 * 2 + (yc + o) % 2
+        share = zeta.at[:, peer // 4, pl.ds(peer % 4 * 2, 2)]
+        send(share, parts.at[o], t_send.at[0], t_recv.at[0], b, cd_of(zh, peer))
+
+    late_start(0, 3, 6)
+    late_start(1, 0, 3)
+    multiply_late(0, 0, 6)
     late_to_tiles(0)
-
+    late_start(1, 3, 6)
     arrive(parts.at[pl.ds(1, 7)], t_recv.at[0])
     total = zeta[:, yc // 4, pl.ds(yc % 4 * 2, 2)]
     for o in range(1, 8):
@@ -264,11 +269,9 @@
         peer = blk_at(o)
         send(summed.at[peer], pieces.at[o], t_send.at[1], t_recv.at[1], peer, c)
 
-    multiply_late(1, 0, LATE_STEPS[1] - 1)
+    multiply_late(1, 0, 6)
+    late_to_tiles(1)
     late_to_all(0)
-    multiply_late(1, LATE_STEPS[1] - 1, LATE_STEPS[1])
-    late_to_tiles(1)
-
     arrive(pieces.at[pl.ds(1, 7)], t_recv.at[1])
     mine = summed[b]
     for o in range(1, N_BLK):
@@ -294,7 +297,7 @@
     left = halves(columns[pl.ds(0, width), :])
     late_rows(1)
     for a in range(2):
-        out[a] = product(left, halves(spread[a]))
+        out[a] = product(left, halves(spread[a, pl.ds(0, 2 * ROWS), :]))
 
     arrive(whole.at[pl.ds(1, 15)], t_send.at[2])
     for g in range(N_LATE):
@@ -330,7 +333,7 @@
             vmem((N_LATE, N_CD, 2, LATE, 128), f32),
             vmem(singles.shape, f32),
             vmem((128, 128), f32),
-            vmem((2, 2 * ROWS, 128), f32),
+            vmem((2, 2 * ROWS + 8, 128), f32),
             dma((STEPS,)), dma(()), dma(()),
             dma(()), dma((STEPS, 3)), dma((N_LATE, max(LATE_STEPS), 3)),
             dma(()), dma((STEPS,)), dma((STEPS,)),

time: 161 us -> 160 us (level)
  no operation moved by 1% of the time
where the time goes in v4:
time: 160 us
  Pallas kernels  159 us (99%)
    pallas_call x1, Pallas kernels, on_device(): pl.pallas_call(kernel, out_shape=jax.ShapeDtypeStruct((2, width, 2 * ROWS...  159 us

profile of v4, /device:TPU:1, one launch (start us, length us, event | category | flops | bytes accessed | tf_op | source)
XLA Modules:
  0.0 160.0 jit_solution(2365810939214321938)
XLA Ops:
  0.0 0.0 copy-start
  0.0 158.5 %shard_map.46 = f32[2,48,128]{2,1,0:T(8,128)} custom-call(f32[128,36864]{1,0:T(8,128)} %tau.1, f32[32,36864]{1,0:T(8,128)} %integrals.1, f32[128,768]{1,0:T(8,128)} %singles.1), custom_call_target="tpu_custom_call" | custom-call | flops 3623878656 | bytes 25165824 | tf_op jit(solution)/shard_map/pallas_call | solution.py:314
  158.5 0.0 copy-done
  158.5 1.4 bitcast_subtract_fusion
Async XLA Ops:
  0.0 158.5 %copy-start = (f32[128,2,48]{0,2,1:T(8,128)S(1)}, f32[128,2,48]{0,2,1:T(8,128)}, u32[]{:S(2)}) copy-start(f32[128,2,48]{0,2,1:T(8,128)} %param.7) | copy-start | bytes 147460

commit v5 on v4

--- a/solution.py
+++ b/solution.py
@@ -10,6 +10,7 @@
 ROWS, KA = 64, 32
 LATE, N_LATE = 8, 2
 EARLY = ROWS - LATE * N_LATE
+SHARES = EARLY // 16
 STEPS = 12
 LATE_STEPS = (6, 6)
 OTHERS = ((1, 2), (0, 2), (0, 1))
@@ -252,36 +253,54 @@
     lax.fori_loop(8, 12, multiply_early, 0)
     for o in FAR_YC:
         peer = (yc // 2 + o // 2) % 4 * 2 + (yc + o) % 2
-        share = zeta.at[:, peer // 4, pl.ds(peer % 4 * 2, 2)]
-        send(share, parts.at[o], t_send.at[0], t_recv.at[0], b, cd_of(zh, peer))
+
+        @pl.when(peer % 4 < SHARES)
+        def _():
+            share = zeta.at[:, peer // 4, pl.ds(peer % 4 * 2, 2)]
+            send(share, parts.at[o], t_send.at[0], t_recv.at[0], b, cd_of(zh, peer))
 
     late_start(0, 3, 6)
     late_start(1, 0, 3)
     multiply_late(0, 0, 6)
     late_to_tiles(0)
     late_start(1, 3, 6)
-    arrive(parts.at[pl.ds(1, 7)], t_recv.at[0])
-    total = zeta[:, yc // 4, pl.ds(yc % 4 * 2, 2)]
-    for o in range(1, 8):
-        total = total + parts[o]
-    summed[...] = total
-    for o in FAR_BLK:
-        peer = blk_at(o)
-        send(summed.at[peer], pieces.at[o], t_send.at[1], t_recv.at[1], peer, c)
+    sharing = yc % 4 < SHARES
+
+    @pl.when(sharing)
+    def _():
+        arrive(parts.at[pl.ds(1, 7)], t_recv.at[0])
+        total = zeta[:, yc // 4, pl.ds(yc % 4 * 2, 2)]
+        for o in range(1, 8):
+            total = total + parts[o]
+        summed[...] = total
+        for o in FAR_BLK:
+            peer = blk_at(o)
+            send(summed.at[peer], pieces.at[o], t_send.at[1], t_recv.at[1], peer, c)
 
     multiply_late(1, 0, 6)
     late_to_tiles(1)
     late_to_all(0)
-    arrive(pieces.at[pl.ds(1, 7)], t_recv.at[1])
-    mine = summed[b]
-    for o in range(1, N_BLK):
-        mine = mine + pieces[o]
-    whole[c] = mine
-    for o in FAR_CD:
-        send(whole.at[c], whole.at[c], t_send.at[2], t_recv.at[2], b, cd_at(o))
+
+    @pl.when(sharing)
+    def _():
+        arrive(pieces.at[pl.ds(1, 7)], t_recv.at[1])
+        mine = summed[b]
+        for o in range(1, N_BLK):
+            mine = mine + pieces[o]
+        whole[c] = mine
+        for o in FAR_CD:
+            send(whole.at[c], whole.at[c], t_send.at[2], t_recv.at[2], b, cd_at(o))
 
     late_to_all(1)
-    arrive(whole.at[pl.ds(1, 15)], t_recv.at[2])
+
+    @pl.when(sharing)
+    def _():
+        arrive(whole.at[pl.ds(0, 4 * SHARES - 1)], t_recv.at[2])
+
+    @pl.when(jnp.logical_not(sharing))
+    def _():
+        arrive(whole.at[pl.ds(0, 4 * SHARES)], t_recv.at[2])
+
     for a in range(2):
         for i in range(EARLY // 8):
             rows = whole[cd_of(0, a * 4 + i // 2), i % 2] + whole[cd_of(1, a * 4 + i // 2), i % 2]
@@ -292,14 +311,21 @@
     arrive(slabs.at[:, :, pl.ds(0, 7)], b_send)
     arrive(early.at[:, :, pl.ds(0, 3)], a_send)
     arrive(late.at[:, :, :, pl.ds(0, 3)], a_send)
-    arrive(parts.at[pl.ds(1, 7)], t_send.at[0])
-    arrive(pieces.at[pl.ds(1, 7)], t_send.at[1])
     left = halves(columns[pl.ds(0, width), :])
     late_rows(1)
     for a in range(2):
         out[a] = product(left, halves(spread[a, pl.ds(0, 2 * ROWS), :]))
 
-    arrive(whole.at[pl.ds(1, 15)], t_send.at[2])
+    @pl.when(sharing)
+    def _():
+        arrive(parts.at[pl.ds(0, 2 * SHARES - 1)], t_send.at[0])
+        arrive(pieces.at[pl.ds(1, 7)], t_send.at[1])
+        arrive(whole.at[pl.ds(1, 15)], t_send.at[2])
+
+    @pl.when(jnp.logical_not(sharing))
+    def _():
+        arrive(parts.at[pl.ds(0, 2 * SHARES)], t_send.at[0])
+
     for g in range(N_LATE):
         arrive(tiles.at[g, pl.ds(1, 7)], t_send.at[3 + g])
         arrive(spreads.at[g, pl.ds(1, 15)], t_send.at[3 + N_LATE + g])

time: 160 us -> 160 us (level)
  no operation moved by 1% of the time
where the time goes in v5:
time: 160 us
  Pallas kernels  158 us (99%)
    pallas_call x1, Pallas kernels, on_device(): pl.pallas_call(kernel, out_shape=jax.ShapeDtypeStruct((2, width, 2 * ROWS...  158 us

profile of v5, /device:TPU:1, one launch (start us, length us, event | category | flops | bytes accessed | tf_op | source)
XLA Modules:
  0.0 159.8 jit_solution(3913210420821458033)
XLA Ops:
  0.0 0.0 copy-start
  0.0 158.4 %shard_map.46 = f32[2,48,128]{2,1,0:T(8,128)} custom-call(f32[128,36864]{1,0:T(8,128)} %tau.1, f32[32,36864]{1,0:T(8,128)} %integrals.1, f32[128,768]{1,0:T(8,128)} %singles.1), custom_call_target="tpu_custom_call" | custom-call | flops 3623878656 | bytes 25165824 | tf_op jit(solution)/shard_map/pallas_call | solution.py:340
  158.4 0.0 copy-done
  158.4 1.4 bitcast_subtract_fusion
Async XLA Ops:
  0.0 158.4 %copy-start = (f32[128,2,48]{0,2,1:T(8,128)S(1)}, f32[128,2,48]{0,2,1:T(8,128)}, u32[]{:S(2)}) copy-start(f32[128,2,48]{0,2,1:T(8,128)} %param.7) | copy-start | bytes 147460
